TPU v7x, 128 devices: a whole 4x4x4 slice. The times are simulated.
128 devices in a mesh: grp: 4 (over z), gx: 32 (over y, x, core).
Axes of the slice: x: 4, y: 4, z: 4, core: 2. Of those that a mesh axis runs over, the one named last changes fastest.
Arguments:
- component_density: float32 [53, 1024, 1024], P(None, 'gx', 'grp'), may hold values from 0.05 to 2
- scaled_thermal_state: float32 [1024, 1024], P('gx', 'grp'), may hold values from 0.5 to 1.5
- leading_direction_flow: float32 [1024, 1024], P('gx', 'grp'), may hold values from -1 to 1
- trailing_direction_flow: float32 [1024, 1024], P('gx', 'grp'), may hold values from -1 to 1
- spreading_coefficient: float32 [54], replicated, may hold values from 0.02 to 0.2
- colliding_pair: int32 [325, 2], replicated, may hold values from 0 to 52
- natural_exponent_scaler: float32 [325], replicated, may hold values from -3 to -1
- arrhenius_energy: float32 [325], replicated, may hold values from 0 to 2
- stoichiometric_output: float32 [325, 53], replicated, may hold values from 0.004 to 0.075
- formation_warming: float32 [53], replicated, may hold values from -1.8 to 1.8
- explicit_increments: int32 [8192], P(('grp', 'gx')), may hold values from 1 to 4
Outputs:
- species_out: float32 [53, 1024, 1024], P(None, 'gx', 'grp')
- temperature_out: float32 [1024, 1024], P('gx', 'grp')
All inputs are finite; a program needn't handle non-finite values.
Results may differ from a plain program's by a relative error of at most 0.0003.
Values sent between devices are 32-bit elements; how exact they have to be, the bound alone decides.
No kernel may reach another device: no remote copies, remote signals or barrier semaphores. Data moves between devices by JAX's collectives and lax.ppermute only.
A program may use at most 64 MiB of HBM per device.

v0:
```python
import math

import jax
import jax.numpy as jnp
from jax import lax
from jax.sharding import Mesh
from jax.sharding import PartitionSpec as P

TILE = 128
GRP_GX = ("grp", "gx_0", "gx_1", "gx_2")
GX = ("gx_0", "gx_1", "gx_2")


transport_step = 0.4
chemistry_span = 0.5
group_tiles = 4
sixth_first = (0.75, -0.15, 1.0 / 60.0)
sixth_second = (1.5, -0.15, 1.0 / 90.0)
sixth_center = -49.0 / 18.0


def extended_2(value, sides, width):
    for axis, dim in sides:
        devices, length = (lax.axis_size(axis), value.shape[dim])
        up = [(i, (i + 1) % devices) for i in range(devices)]
        down = [(j, i) for i, j in up]
        last = lax.slice_in_dim(value, length - width, length, axis=dim)
        initial = lax.slice_in_dim(value, 0, width, axis=dim)
        before = lax.ppermute(last, axis, up)
        after = lax.ppermute(initial, axis, down)
        value = jnp.concatenate([before, value, after], axis=dim)
    return value


def in_blocks(value, dim, devices):
    shape = value.shape
    tiles = value.reshape(*shape[:dim], devices, shape[dim] // devices, *shape[dim + 1 :])
    return jnp.moveaxis(tiles, dim, 0)


def joined_along(tiles, dim):
    shape = list(tiles.shape[1:])
    shape[dim] *= tiles.shape[0]
    return jnp.moveaxis(tiles, 0, dim).reshape(shape)


def moved_by_axis(tiles, axes, sequence):
    inside = tiles.shape[1:]
    out = tiles.reshape(*(lax.axis_size(a) for a in axes), *inside)
    for k in sequence:
        out = lax.all_to_all(out, axes[k], k, k, tiled=True)
    return out.reshape(-1, *inside)


def two_step_exchange(value, groups, sequence, split_dim, concat_dim):
    devices = lax.axis_size(groups[0]) * lax.axis_size(groups[1])
    tiles = in_blocks(value, split_dim, devices)
    return joined_along(moved_by_axis(tiles, groups, sequence), concat_dim)


def tendency(extended, speeds, spreading_coefficient):
    height = extended.shape[1] - 6
    breadth = extended.shape[2] - 6

    def along_first(values, offset):
        return values[:, 3 + offset : 3 + offset + height, 3 : 3 + breadth]

    def along_second(values, offset):
        return values[:, 3 : 3 + height, 3 + offset : 3 + offset + breadth]

    east_flux = speeds[0:1] * extended
    north_flux = speeds[1:2] * extended
    gradient = jnp.zeros((extended.shape[0], height, breadth), jnp.float32)
    laplacian = 2.0 * sixth_center * along_first(extended, 0)
    for offset in range(1, 4):
        gradient = gradient + sixth_first[offset - 1] * (
            along_first(east_flux, offset)
            - along_first(east_flux, -offset)
            + along_second(north_flux, offset)
            - along_second(north_flux, -offset)
        )
        laplacian = laplacian + sixth_second[offset - 1] * (
            along_first(extended, offset)
            + along_first(extended, -offset)
            + along_second(extended, offset)
            + along_second(extended, -offset)
        )
    return spreading_coefficient[:, None, None] * laplacian - gradient


def build_tables(colliding_pair, stoichiometric_output):
    species_ids = jnp.arange(stoichiometric_output.shape[1], dtype=jnp.int32)[:, None]
    first_table = (species_ids == colliding_pair[None, :, 0]).astype(jnp.float32)
    second_table = (species_ids == colliding_pair[None, :, 1]).astype(jnp.float32)
    return (stoichiometric_output.T, jnp.concatenate([first_table, second_table], 1))


def substep_once(combined_state_array, step_sizes, mechanism):
    (
        gain_table,
        loss_table,
        colliding_pair,
        natural_exponent_scaler,
        arrhenius_energy,
        formation_warming,
    ) = mechanism
    amounts = combined_state_array[:-1]
    warmth = combined_state_array[-1]
    rate_constant = jnp.exp(
        natural_exponent_scaler[:, None] + arrhenius_energy[:, None] * jnp.tanh(warmth)[None, :]
    )
    first_partner = jnp.take(amounts, colliding_pair[:, 0], axis=0)
    second_partner = jnp.take(amounts, colliding_pair[:, 1], axis=0)
    progress = rate_constant * first_partner * second_partner
    gained = jnp.dot(
        gain_table, progress, precision=lax.Precision.HIGHEST, preferred_element_type=jnp.float32
    )
    partners = jnp.concatenate([rate_constant * second_partner, rate_constant * first_partner], 0)
    destroyed = jnp.dot(
        loss_table, partners, precision=lax.Precision.HIGHEST, preferred_element_type=jnp.float32
    )
    updated = (amounts + step_sizes[None, :] * gained) / (1.0 + step_sizes[None, :] * destroyed)
    warmer = warmth + jnp.dot(
        formation_warming,
        updated - amounts,
        precision=lax.Precision.HIGHEST,
        preferred_element_type=jnp.float32,
    )
    return jnp.concatenate([updated, warmer[None, :]], 0)


def substep_loop(combined_state_array, counts, turn_count, mechanism):
    step_sizes = chemistry_span / counts.astype(jnp.float32)

    def advance(substep, current):
        advanced = substep_once(current, step_sizes, mechanism)
        return jnp.where((substep < counts)[None, :], advanced, current)

    return lax.fori_loop(0, turn_count, advance, combined_state_array)


def integrate(tile_rows, counts, mechanism):
    layers = tile_rows.shape[0]
    number = tile_rows.shape[1]
    group_size = math.gcd(number, group_tiles)
    ranking = jnp.argsort(counts, stable=True)
    inverse = jnp.argsort(ranking, stable=True)
    ranked = jnp.take(tile_rows, ranking, axis=1)
    ranked_counts = jnp.take(counts, ranking)

    def handle(group_index, finished):
        offset_at = group_index * group_size
        tile_block = lax.dynamic_slice_in_dim(ranked, offset_at, group_size, 1).reshape(
            layers, group_size * TILE
        )
        block_counts = lax.dynamic_slice_in_dim(ranked_counts, offset_at, group_size, 0)
        turn_count = jnp.max(block_counts)
        cell_counts = jnp.repeat(block_counts, TILE)
        result = substep_loop(tile_block, cell_counts, turn_count, mechanism)
        return lax.dynamic_update_slice_in_dim(
            finished, result.reshape(layers, group_size, TILE), offset_at, 1
        )

    finished = lax.fori_loop(0, number // group_size, handle, jnp.zeros_like(ranked))
    return jnp.take(finished, inverse, axis=1)


def body(
    component_density,
    scaled_thermal_state,
    leading_direction_flow,
    trailing_direction_flow,
    spreading_coefficient,
    colliding_pair,
    natural_exponent_scaler,
    arrhenius_energy,
    stoichiometric_output,
    formation_warming,
    explicit_increments,
):
    combined_state_array = jnp.concatenate([component_density, scaled_thermal_state[None]], 0)
    speeds = jnp.stack([leading_direction_flow, trailing_direction_flow])
    bundle = jnp.concatenate([combined_state_array, speeds], 0)
    layers = combined_state_array.shape[0]
    widened = extended_2(bundle, (("grp", 2), (GX, 1)), 9)
    start_field = widened[:layers]
    speed_wide = widened[layers:]
    center = start_field[:, 3:-3, 3:-3]
    section_one = center + transport_step * tendency(start_field, speed_wide, spreading_coefficient)
    section_two = 0.75 * center[:, 3:-3, 3:-3] + 0.25 * (
        section_one[:, 3:-3, 3:-3]
        + transport_step * tendency(section_one, speed_wide[:, 3:-3, 3:-3], spreading_coefficient)
    )
    advected = center[:, 6:-6, 6:-6] / 3.0 + 2.0 / 3.0 * (
        section_two[:, 3:-3, 3:-3]
        + transport_step * tendency(section_two, speed_wide[:, 6:-6, 6:-6], spreading_coefficient)
    )
    clipped = jnp.concatenate([jnp.maximum(advected[:-1], 0.0), advected[-1:]], 0)
    tile_rows = clipped.reshape(layers, -1, TILE)
    gain_table, loss_table = build_tables(colliding_pair, stoichiometric_output)
    mechanism = (
        gain_table,
        loss_table,
        colliding_pair,
        natural_exponent_scaler,
        arrhenius_energy,
        formation_warming,
    )
    peer_count = lax.axis_size(GX)
    spread = tile_rows.reshape(layers, peer_count, -1, TILE)
    tallies = explicit_increments.astype(jnp.float32).reshape(1, peer_count, -1, 1)
    pieces = two_step_exchange(spread, (("gx_0", "gx_1"), "gx_2"), (0, 1), 1, 1)
    marks = two_step_exchange(tallies, (("gx_0", "gx_1"), "gx_2"), (0, 1), 1, 1)
    shape_now = pieces.shape
    worked = integrate(
        pieces.reshape(layers, -1, TILE), marks.reshape(-1).astype(jnp.int32), mechanism
    )
    reacted = lax.all_to_all(
        worked.reshape(shape_now), GX, split_axis=1, concat_axis=1, tiled=True
    ).reshape(layers, -1, TILE)
    restored = reacted.reshape(layers, component_density.shape[1], component_density.shape[2])
    return (restored[:-1], restored[-1])


def solution(mesh):
    finer = Mesh(mesh.devices.reshape(mesh.shape["grp"], 4, 4, 2), ("grp", "gx_0", "gx_1", "gx_2"))
    return jax.shard_map(
        body,
        mesh=finer,
        in_specs=(
            P(None, GX, "grp"),
            P(GX, "grp"),
            P(GX, "grp"),
            P(GX, "grp"),
            P(),
            P(),
            P(),
            P(),
            P(),
            P(),
            P(GRP_GX),
        ),
        out_specs=(P(None, GX, "grp"), P(GX, "grp")),
        check_vma=False,
    )
```

profile of v0, /device:TPU:97, one launch (start us, length us, event | category | flops | bytes accessed | tf_op | source)
XLA Modules:
  0.0 488.2 jit_solution(11853201831407491891)
XLA Ops:
  3.6 1.7 copy.38
  7.4 2.6 collective-permute-done
  11.9 1.7 copy.41
  13.6 2.3 pad_maximum_fusion.1
  16.3 2.7 collective-permute-start.2
  20.3 13.0 %all_to_all.25 = f32[16,2,1,1,2,1]{4,1,5,3,2,0:T(2,128)S(1)} all-to-all(f32[16,2,1,1,2,1]{4,1,5,3,2,0:T(2,128)S(1)} %bitcast.117), channel_id=1, replica_groups=mesh['grp'=4,'gx_0'=4,'gx_1'=4,'gx_2'=2] {'gx_0','gx_1'}, dimensions={0} | all-to-all | bytes 512 | tf_op jit(solution)/shard_map/all_to_all | solution.py:51
  34.1 5.4 %all-to-all-start.3 = ((f32[16,2,1,1,2,1]{0,4,5,3,2,1:T(2,128)}), f32[16,2,1,1,2,1]{0,4,5,3,2,1:T(2,128)S(1)}, u32[]{:S(2)}, u32[]{:S(2)}) async-start(f32[16,2,1,1,2,1]{0,4,5,3,2,1:T(2,128)} %copy.36), calls=%async_computation.3 | async-start | bytes 4096 | tf_op jit(solution)/shard_map/all_to_all | solution.py:51
  41.0 7.2 %pad_maximum_fusion = f32[56,50,274]{2,1,0:T(8,128)S(1)} fusion(f32[56,9,274]{2,1,0:T(8,128)S(1)} %copy.45, f32[56,32,9]{2,1,0:T(8,128)} %copy.41, f32[1,32,256]{2,1,0:T(8,128)S(1)} %bitcast.113, f32[1,32,256]{2,1,0:T(8,128)S(1)} %bitcast.116, f32[1,32,256]{2,1,0:T(8,128)S(1)} %bitcast.109, f32[53,32,256]{2,1,0:T(8,128)S(1)} %copy-done.3, ...), kind=kLoop, calls=%fused_computation.46 | loop fusion | flops 5370400 | bytes 6137600 | tf_op jit(solution)/shard_map/concatenate | solution.py:31
  48.5 4.1 slice_multiply_fusion.1
  52.6 36.8 %broadcast_multiply_fusion.1 = (f32[54,44,268]{2,1,0:T(8,128)}, f32[54,44,268]{2,1,0:T(8,128)}) fusion(f32[44,268]{1,0:T(8,128)S(1)} %get-tuple-element.385, f32[54,50,274]{2,1,0:T(8,128)} %get-tuple-element.387, f32[54,50,274]{2,1,0:T(8,128)} %get-tuple-element.386, f32[56,50,274]{2,1,0:T(8,128)S(1)} %pad_maximum_fusion, f32[54]{0:T(128)S(1)} %copy-done.14), kind=kLoop, calls=%fused_computation.120 | loop fusion | flops 22286880 | bytes 68818328 | tf_op jit(solution)/shard_map/mul | solution.py:71
  89.5 4.5 broadcast_multiply_fusion
  94.0 33.1 %broadcast_multiply_fusion.3 = (f32[54,38,262]{2,1,0:T(8,128)}, f32[54,38,262]{2,1,0:T(8,128)}) fusion(f32[38,262]{1,0:T(8,128)S(1)} %get-tuple-element.383, f32[54,44,268]{2,1,0:T(8,128)} %broadcast_multiply_fusion, f32[54,44,268]{2,1,0:T(8,128)} %get-tuple-element.372, f32[54,44,268]{2,1,0:T(8,128)S(1)} %copy-done, f32[54]{0:T(128)S(1)} %copy-done.14, ...), kind=kLoop, calls=%fused_computation.162 | loop fusion | flops 20429712 | bytes 60253928 | tf_op jit(solution)/shard_map/mul | solution.py:71
  127.1 4.0 broadcast_multiply_fusion.2
  131.0 22.7 %fusion.70 = f32[54,32,256]{2,1,0:T(8,128)} fusion(f32[54,38,262]{2,1,0:T(8,128)} %broadcast_multiply_fusion.2, f32[54,38,262]{2,1,0:T(8,128)} %get-tuple-element.370, f32[54,38,262]{2,1,0:T(8,128)S(1)} %copy-done.1, f32[1,32,256]{2,1,0:T(8,128)S(1)} %bitcast.110, f32[53,32,256]{2,1,0:T(8,128)} %param.19, f32[54]{0:T(128)S(1)} %copy-done.14), kind=kLoop, calls=%fused_computation.130 | loop fusion | flops 16809984 | bytes 47775960 | tf_op jit(solution)/shard_map/add | solution.py:194
  156.4 1.8 copy.46
  158.3 6.0 %all-to-all-start = ((f32[16,2,54,1,2,128]{5,4,3,2,1,0:T(2,128)}), f32[16,2,54,1,2,128]{5,4,3,2,1,0:T(2,128)S(1)}, u32[]{:S(2)}, u32[]{:S(2)}) async-start(f32[16,2,54,1,2,128]{5,4,3,2,1,0:T(2,128)} %bitcast.11), calls=%async_computation | async-start | bytes 3538944 | tf_op jit(solution)/shard_map/all_to_all | solution.py:51
  164.7 2.0 sort.31
  167.5 2.0 sort.32
  169.6 23.4 %all-to-all-done = f32[16,2,54,1,2,128]{5,4,3,2,1,0:T(2,128)S(1)} async-done(((f32[16,2,54,1,2,128]{5,4,3,2,1,0:T(2,128)}), f32[16,2,54,1,2,128]{5,4,3,2,1,0:T(2,128)S(1)}, u32[]{:S(2)}, u32[]{:S(2)}) %all-to-all-start) | async-done | bytes 1769504 | tf_op jit(solution)/shard_map/all_to_all | solution.py:51
  193.3 5.9 %all_to_all.26 = f32[16,2,54,1,2,128]{5,0,4,3,2,1:T(8,128)S(1)} all-to-all(f32[16,2,54,1,2,128]{5,0,4,3,2,1:T(8,128)S(1)} %copy.47), channel_id=1, replica_groups=mesh['grp'=4,'gx_0'=4,'gx_1'=4,'gx_2'=2] {'gx_2'}, dimensions={1} | all-to-all | bytes 3538944 | tf_op jit(solution)/shard_map/all_to_all | solution.py:51
  201.8 1.9 gather_fusion.3
  203.8 1.7 select_bitcast_fusion
  207.3 238.1 %while.38 = (s32[]{:T(128)}, f32[54,64,128]{2,1,0:T(8,128)S(1)}, f32[54,64,128]{2,1,0:T(8,128)}, s32[64]{0:T(128)S(1)}, f32[325]{0:T(512)S(1)}, /*index=5*/f32[3...) while((s32[]{:T(128)}, f32[54,64,128]{2,1,0:T(8,128)S(1)}, ...), condition=%wide.region_5.8_spmd, body=%wide.region_1.7_spmd.sunk | while | flops 319708896 | bytes 10352105 | solution.py:164
  209.0 7.0 %while.39 = (s32[]{:T(128)}, f32[54,512]{1,0:T(8,128)S(1)}, s32[]{:T(128)}, f32[325]{0:T(512)S(1)}, f32[325]{0:T(512)S(1)}, /*index=5*/s32[325,2]{0,1:T(2,128)S(...) while((s32[]{:T(128)}, f32[54,512]{1,0:T(8,128)S(1)}, ...), condition=%wide.region_4.6_spmd.clone.clone, body=%wide.region_3.5_spmd.clone.clone.sunk | while | flops 319708896 | bytes 9233514 | solution.py:139
  209.6 1.7 gather_fusion
  211.3 1.7 gather_fusion.1
  217.8 7.0 %while.39 = (s32[]{:T(128)}, f32[54,512]{1,0:T(8,128)S(1)}, s32[]{:T(128)}, f32[325]{0:T(512)S(1)}, f32[325]{0:T(512)S(1)}, /*index=5*/s32[325,2]{0,1:T(2,128)S(...) while((s32[]{:T(128)}, f32[54,512]{1,0:T(8,128)S(1)}, ...), condition=%wide.region_4.6_spmd.clone.clone, body=%wide.region_3.5_spmd.clone.clone.sunk | while | flops 319708896 | bytes 9233514 | solution.py:139
  218.4 1.7 gather_fusion
  226.6 7.0 %while.39 = (s32[]{:T(128)}, f32[54,512]{1,0:T(8,128)S(1)}, s32[]{:T(128)}, f32[325]{0:T(512)S(1)}, f32[325]{0:T(512)S(1)}, /*index=5*/s32[325,2]{0,1:T(2,128)S(...) while((s32[]{:T(128)}, f32[54,512]{1,0:T(8,128)S(1)}, ...), condition=%wide.region_4.6_spmd.clone.clone, body=%wide.region_3.5_spmd.clone.clone.sunk | while | flops 319708896 | bytes 9233514 | solution.py:139
  235.5 7.0 %while.39 = (s32[]{:T(128)}, f32[54,512]{1,0:T(8,128)S(1)}, s32[]{:T(128)}, f32[325]{0:T(512)S(1)}, f32[325]{0:T(512)S(1)}, /*index=5*/s32[325,2]{0,1:T(2,128)S(...) while((s32[]{:T(128)}, f32[54,512]{1,0:T(8,128)S(1)}, ...), condition=%wide.region_4.6_spmd.clone.clone, body=%wide.region_3.5_spmd.clone.clone.sunk | while | flops 319708896 | bytes 9233514 | solution.py:139
  244.3 13.5 %while.39 = (s32[]{:T(128)}, f32[54,512]{1,0:T(8,128)S(1)}, s32[]{:T(128)}, f32[325]{0:T(512)S(1)}, f32[325]{0:T(512)S(1)}, /*index=5*/s32[325,2]{0,1:T(2,128)S(...) while((s32[]{:T(128)}, f32[54,512]{1,0:T(8,128)S(1)}, ...), condition=%wide.region_4.6_spmd.clone.clone, body=%wide.region_3.5_spmd.clone.clone.sunk | while | flops 319708896 | bytes 9233514 | solution.py:139
  259.6 13.5 %while.39 = (s32[]{:T(128)}, f32[54,512]{1,0:T(8,128)S(1)}, s32[]{:T(128)}, f32[325]{0:T(512)S(1)}, f32[325]{0:T(512)S(1)}, /*index=5*/s32[325,2]{0,1:T(2,128)S(...) while((s32[]{:T(128)}, f32[54,512]{1,0:T(8,128)S(1)}, ...), condition=%wide.region_4.6_spmd.clone.clone, body=%wide.region_3.5_spmd.clone.clone.sunk | while | flops 319708896 | bytes 9233514 | solution.py:139
  274.8 13.5 %while.39 = (s32[]{:T(128)}, f32[54,512]{1,0:T(8,128)S(1)}, s32[]{:T(128)}, f32[325]{0:T(512)S(1)}, f32[325]{0:T(512)S(1)}, /*index=5*/s32[325,2]{0,1:T(2,128)S(...) while((s32[]{:T(128)}, f32[54,512]{1,0:T(8,128)S(1)}, ...), condition=%wide.region_4.6_spmd.clone.clone, body=%wide.region_3.5_spmd.clone.clone.sunk | while | flops 319708896 | bytes 9233514 | solution.py:139
  290.1 13.5 %while.39 = (s32[]{:T(128)}, f32[54,512]{1,0:T(8,128)S(1)}, s32[]{:T(128)}, f32[325]{0:T(512)S(1)}, f32[325]{0:T(512)S(1)}, /*index=5*/s32[325,2]{0,1:T(2,128)S(...) while((s32[]{:T(128)}, f32[54,512]{1,0:T(8,128)S(1)}, ...), condition=%wide.region_4.6_spmd.clone.clone, body=%wide.region_3.5_spmd.clone.clone.sunk | while | flops 319708896 | bytes 9233514 | solution.py:139
  305.4 13.5 %while.39 = (s32[]{:T(128)}, f32[54,512]{1,0:T(8,128)S(1)}, s32[]{:T(128)}, f32[325]{0:T(512)S(1)}, f32[325]{0:T(512)S(1)}, /*index=5*/s32[325,2]{0,1:T(2,128)S(...) while((s32[]{:T(128)}, f32[54,512]{1,0:T(8,128)S(1)}, ...), condition=%wide.region_4.6_spmd.clone.clone, body=%wide.region_3.5_spmd.clone.clone.sunk | while | flops 319708896 | bytes 9233514 | solution.py:139
  320.7 13.5 %while.39 = (s32[]{:T(128)}, f32[54,512]{1,0:T(8,128)S(1)}, s32[]{:T(128)}, f32[325]{0:T(512)S(1)}, f32[325]{0:T(512)S(1)}, /*index=5*/s32[325,2]{0,1:T(2,128)S(...) while((s32[]{:T(128)}, f32[54,512]{1,0:T(8,128)S(1)}, ...), condition=%wide.region_4.6_spmd.clone.clone, body=%wide.region_3.5_spmd.clone.clone.sunk | while | flops 319708896 | bytes 9233514 | solution.py:139
  336.0 13.5 %while.39 = (s32[]{:T(128)}, f32[54,512]{1,0:T(8,128)S(1)}, s32[]{:T(128)}, f32[325]{0:T(512)S(1)}, f32[325]{0:T(512)S(1)}, /*index=5*/s32[325,2]{0,1:T(2,128)S(...) while((s32[]{:T(128)}, f32[54,512]{1,0:T(8,128)S(1)}, ...), condition=%wide.region_4.6_spmd.clone.clone, body=%wide.region_3.5_spmd.clone.clone.sunk | while | flops 319708896 | bytes 9233514 | solution.py:139
  351.3 13.5 %while.39 = (s32[]{:T(128)}, f32[54,512]{1,0:T(8,128)S(1)}, s32[]{:T(128)}, f32[325]{0:T(512)S(1)}, f32[325]{0:T(512)S(1)}, /*index=5*/s32[325,2]{0,1:T(2,128)S(...) while((s32[]{:T(128)}, f32[54,512]{1,0:T(8,128)S(1)}, ...), condition=%wide.region_4.6_spmd.clone.clone, body=%wide.region_3.5_spmd.clone.clone.sunk | while | flops 319708896 | bytes 9233514 | solution.py:139
  366.5 13.5 %while.39 = (s32[]{:T(128)}, f32[54,512]{1,0:T(8,128)S(1)}, s32[]{:T(128)}, f32[325]{0:T(512)S(1)}, f32[325]{0:T(512)S(1)}, /*index=5*/s32[325,2]{0,1:T(2,128)S(...) while((s32[]{:T(128)}, f32[54,512]{1,0:T(8,128)S(1)}, ...), condition=%wide.region_4.6_spmd.clone.clone, body=%wide.region_3.5_spmd.clone.clone.sunk | while | flops 319708896 | bytes 9233514 | solution.py:139
  381.8 13.5 %while.39 = (s32[]{:T(128)}, f32[54,512]{1,0:T(8,128)S(1)}, s32[]{:T(128)}, f32[325]{0:T(512)S(1)}, f32[325]{0:T(512)S(1)}, /*index=5*/s32[325,2]{0,1:T(2,128)S(...) while((s32[]{:T(128)}, f32[54,512]{1,0:T(8,128)S(1)}, ...), condition=%wide.region_4.6_spmd.clone.clone, body=%wide.region_3.5_spmd.clone.clone.sunk | while | flops 319708896 | bytes 9233514 | solution.py:139
  397.1 19.9 %while.39 = (s32[]{:T(128)}, f32[54,512]{1,0:T(8,128)S(1)}, s32[]{:T(128)}, f32[325]{0:T(512)S(1)}, f32[325]{0:T(512)S(1)}, /*index=5*/s32[325,2]{0,1:T(2,128)S(...) while((s32[]{:T(128)}, f32[54,512]{1,0:T(8,128)S(1)}, ...), condition=%wide.region_4.6_spmd.clone.clone, body=%wide.region_3.5_spmd.clone.clone.sunk | while | flops 319708896 | bytes 9233514 | solution.py:139
  418.9 26.4 %while.39 = (s32[]{:T(128)}, f32[54,512]{1,0:T(8,128)S(1)}, s32[]{:T(128)}, f32[325]{0:T(512)S(1)}, f32[325]{0:T(512)S(1)}, /*index=5*/s32[325,2]{0,1:T(2,128)S(...) while((s32[]{:T(128)}, f32[54,512]{1,0:T(8,128)S(1)}, ...), condition=%wide.region_4.6_spmd.clone.clone, body=%wide.region_3.5_spmd.clone.clone.sunk | while | flops 319708896 | bytes 9233514 | solution.py:139
  446.6 2.5 copy.51
  449.1 1.9 gather_fusion.4
  451.1 1.7 broadcast_select_fusion
  453.7 26.5 %all_to_all.27 = f32[54,32,2,128]{3,2,0,1:T(2,128)S(1)} all-to-all(f32[54,32,2,128]{3,2,0,1:T(2,128)S(1)} %copy.52), channel_id=1, replica_groups=mesh['grp'=4,'gx_0'=4,'gx_1'=4,'gx_2'=2] {'gx_0','gx_1','gx_2'}, dimensions={1} | all-to-all | bytes 3538944 | tf_op jit(solution)/shard_map/all_to_all | solution.py:218
  482.8 2.7 reshape.130
  485.4 1.7 copy.54
  (673 shorter events, 228.2 us)
Async XLA Ops:
  2.3 11.3 %copy-start.3 = (f32[53,32,256]{2,1,0:T(8,128)S(1)}, f32[53,32,256]{2,1,0:T(8,128)}, u32[]{:S(2)}) copy-start(f32[53,32,256]{2,1,0:T(8,128)} %param.19) | copy-start | bytes 5210116
  2.3 11.3 %copy-start.10 = (f32[32,256]{1,0:T(8,128)S(1)}, f32[32,256]{1,0:T(8,128)}, u32[]{:S(2)}) copy-start(f32[32,256]{1,0:T(8,128)} %param.20) | copy-start | bytes 98308
  2.3 11.3 %copy-start.12 = (f32[32,256]{1,0:T(8,128)S(1)}, f32[32,256]{1,0:T(8,128)}, u32[]{:S(2)}) copy-start(f32[32,256]{1,0:T(8,128)} %param.22) | copy-start | bytes 98308
  2.3 11.3 %copy-start.13 = (f32[32,256]{1,0:T(8,128)S(1)}, f32[32,256]{1,0:T(8,128)}, u32[]{:S(2)}) copy-start(f32[32,256]{1,0:T(8,128)} %param.21) | copy-start | bytes 98308
  5.3 4.8 collective-permute-start
  5.9 6.0 %collective-permute-start.1 = (f32[56,32,9]{0,1,2:T(8,128)S(1)}, f32[56,32,9]{0,1,2:T(8,128)S(1)}, u32[]{:S(2)}, u32[]{:S(2)}) collective-permute-start(f32[56,32,9]{0,1,2:T(8,128)S(1)} %copy.39), channel_id=1, source_target_pairs={{32,0},{64,32},{96,64},{0,96},{33,1},{65,33},{97,65},{1,97},{34,2}... | collective-permute-start | bytes 193544 | tf_op jit(solution)/shard_map/ppermute | solution.py:30
  10.9 4.9 %copy-start.4 = (f32[56,32,9]{2,1,0:T(8,128)}, f32[56,32,9]{2,1,0:T(8,128)S(1)}, u32[]{:S(2)}) copy-start(f32[56,32,9]{2,1,0:T(8,128)S(1)} %copy.40) | copy-start | bytes 193540
  16.1 4.1 copy-start.15
  16.3 23.1 %collective-permute-start.2 = (f32[56,9,274]{2,0,1:T(8,128)S(1)}, f32[56,9,274]{2,0,1:T(8,128)S(1)}, u32[]{:S(2)}, u32[]{:S(2)}) collective-permute-start(f32[56,9,274]{2,0,1:T(8,128)S(1)} %copy.42), channel_id=1, source_target_pairs={{0,1},{1,2},{2,3},{3,4},{4,5},{5,6},{6,7},{7,8},{8,9},{9,10},{10,1... | collective-permute-start | bytes 1657160 | tf_op jit(solution)/shard_map/ppermute | solution.py:29
  20.2 19.5 %collective-permute-start.3 = (f32[56,9,274]{2,0,1:T(8,128)}, f32[56,9,274]{2,0,1:T(8,128)}, u32[]{:S(2)}, u32[]{:S(2)}) collective-permute-start(f32[56,9,274]{2,0,1:T(8,128)} %copy.43), channel_id=1, source_target_pairs={{1,0},{2,1},{3,2},{4,3},{5,4},{6,5},{7,6},{8,7},{9,8},{10,9},{11,1... | collective-permute-start | bytes 1657160 | tf_op jit(solution)/shard_map/ppermute | solution.py:30
  34.1 124.2 %all-to-all-start.3 = ((f32[16,2,1,1,2,1]{0,4,5,3,2,1:T(2,128)}), f32[16,2,1,1,2,1]{0,4,5,3,2,1:T(2,128)S(1)}, u32[]{:S(2)}, u32[]{:S(2)}) async-start(f32[16,2,1,1,2,1]{0,4,5,3,2,1:T(2,128)} %copy.36), calls=%async_computation.3 | async-start | bytes 4096 | tf_op jit(solution)/shard_map/all_to_all | solution.py:51
  48.5 4.1 copy-start.14
  89.5 4.5 copy-start
  127.0 4.0 copy-start.1
  153.7 1.6 slice-start.1
  156.4 7.8 %copy-start.7 = (s32[325,2]{0,1:T(2,128)S(1)}, s32[325,2]{0,1:T(2,128)}, u32[]{:S(2)}) copy-start(s32[325,2]{0,1:T(2,128)} %param.24) | copy-start | bytes 7804
  158.3 34.7 %all-to-all-start = ((f32[16,2,54,1,2,128]{5,4,3,2,1,0:T(2,128)}), f32[16,2,54,1,2,128]{5,4,3,2,1,0:T(2,128)S(1)}, u32[]{:S(2)}, u32[]{:S(2)}) async-start(f32[16,2,54,1,2,128]{5,4,3,2,1,0:T(2,128)} %bitcast.11), calls=%async_computation | async-start | bytes 3538944 | tf_op jit(solution)/shard_map/all_to_all | solution.py:51
  205.5 1.8 copy-start.2
  205.5 1.8 copy-start.8
  205.5 1.8 copy-start.9
  205.5 1.8 copy-start.11
  445.4 1.2 copy-start.6
  480.2 1.2 copy-start.5
  482.8 4.4 slice-start
where the time goes:
time: 498 us; the launch traced here: 488 us
  local copies, waits for them, and re-layouts  155 us (31%)
  other arithmetic  151 us (30%)
  matrix products  62.3 us (13%)
  blocking collectives  45.5 us (9%)
  loops' own time  29.9 us (6%)
  waiting for transfers between devices  27 us (5%)
  starting transfers between devices  15.7 us (3%)
    mul x3, other arithmetic, tendency(): east_flux = speeds[0:1] * extended  74 us
    gather x31, local copies, waits for them, and re-layouts, substep_once(): second_partner = jnp.take(amounts, colliding_pair[:, 1], axis=0)  51.2 us
    gather x31, local copies, waits for them, and re-layouts, substep_once(): first_partner = jnp.take(amounts, colliding_pair[:, 0], axis=0)  51.2 us
    dot_general x31, matrix products, substep_once(): jnp.dot(loss_table, partners, precision=lax.Precision.HIGHEST, preferred_...  34.1 us
    another operation x16, loops' own time, substep_loop(): return lax.fori_loop(0, turn_count, advance, combined_state_array)  28.9 us
    all_to_all x1, blocking collectives, body(): lax.all_to_all(worked.reshape(shape_now), GX, split_axis=1, concat_axis=1...  26.5 us
    all_to_all x2, waiting for transfers between devices, moved_by_axis(): out = lax.all_to_all(out, axes[k], k, k, tiled=True)  23.4 us
    add x1, other arithmetic, body(): center[:, 6:-6, 6:-6] / 3.0  22.7 us
  transfers between devices with their start and end apart: 6, of which 3 were waited for; matrix products, arithmetic and copies ran while one was open for 26% of the time, Pallas kernels for 0%

commit v1 on v0

v1 whole, which is shorter than its diff:
```python
import math

import jax
import jax.numpy as jnp
from jax import lax
from jax.experimental import pallas as pl
from jax.experimental.pallas import tpu as pltpu
from jax.sharding import PartitionSpec as P

SPECIES = 53
ROWS = 56
FT = ROWS // 8
CX, CY = 32, 256
TILES = 64
HALO = 9
WIDE = 384
RXN = 336
GROUP = 8
CELLS = GROUP * 128
DT = 0.4
SPAN = 0.5
FIRST = (0.75, -0.15, 1.0 / 60.0)
SECOND = (1.5, -0.15, 1.0 / 90.0)
CENTER = -49.0 / 18.0
FLOOR = 1e-20
F32, BF16 = jnp.float32, jnp.bfloat16


def two_parts(value):
    high = value.astype(BF16).astype(F32)
    return high, value - high


def pack_kernel(density, thermal, lead, trail, own, first, last, edges):
    for b in range(CX // 8):
        for half in range(2):
            for f in range(ROWS):
                source = density if f < SPECIES else (thermal, lead, trail)[f - SPECIES]
                at = (slice(b * 8, b * 8 + 8), slice(half * 128, half * 128 + 128))
                value = source[(f, *at)] if f < SPECIES else source[at]
                row = (b * 8 * 14 + 2 * (f // 8) + half) * 8 + f % 8
                own[pl.ds(row, 8, stride=14 * 8), :] = value
    lane = lax.broadcasted_iota(jnp.int32, (8, 128), 1)

    def at_row(x, _):
        packed = jnp.zeros((8, 128), F32)
        for t in range(FT):
            row = pl.multiple_of((x * 14 + 2 * t) * 8, 8)
            left = pltpu.roll(own[pl.ds(row, 8), :], 9 * t, 1)
            right = pltpu.roll(own[pl.ds(row + 8, 8), :], (63 + 9 * t - 119) % 128, 1)
            packed = jnp.where((lane >= 9 * t) & (lane < 9 * t + 9), left, packed)
            packed = jnp.where((lane >= 63 + 9 * t) & (lane < 72 + 9 * t), right, packed)
        edges[x] = packed
        return 0

    lax.fori_loop(0, CX, at_row, 0, unroll=2)
    first[...] = own[: HALO * 112, :]
    last[...] = own[(CX - HALO) * 112 :, :]


def run_stage(src, base, base_at, diffusion, speeds, speed_at, rows, block, mix, store):
    keep, take = mix

    def at_block(b, _):
        x0 = b * block
        for t in range(FT):
            r = jnp.concatenate([diffusion[t]] * 3, axis=1)
            rk = [(DT * c) * r for c in SECOND]
            rc = (2.0 * DT * CENTER) * r
            f = [src[x0 + i, t] for i in range(block + 6)]
            q = [speeds[0, speed_at + x0 + i] * f[i] for i in range(block + 6)]
            for i in range(block):
                j = i + 3
                v = speeds[1, speed_at + x0 + j] * f[j]
                total, cross = rc * f[j], None
                for k in (1, 2, 3):
                    total = total + rk[k - 1] * (f[j + k] + f[j - k])
                    total = total - FIRST[k - 1] * (q[j + k] - q[j - k])
                    even = rk[k - 1] * f[j]
                    odd = FIRST[k - 1] * v
                    turned = pltpu.roll(even - odd, WIDE - k, 1) + pltpu.roll(even + odd, k, 1)
                    cross = turned if cross is None else cross + turned
                out = f[j] + (total + cross)
                if keep is not None:
                    out = keep * base[base_at + x0 + i, t] + take * out
                store(x0 + i, t, out)
        return 0

    lax.fori_loop(0, rows // block, at_block, 0)


def react_group(g, counts, order, tiles, gathers, sums, warming, done):
    ids = [order[g * GROUP + i] for i in range(GROUP)]
    number = jnp.concatenate([jnp.full((1, 128), counts[i], jnp.int32) for i in ids], axis=1)
    h = SPAN / number.astype(F32)
    row = lax.broadcasted_iota(jnp.int32, (ROWS, CELLS), 0)
    species = row < SPECIES
    state = jnp.concatenate([tiles[i].reshape(ROWS, 128) for i in ids], axis=1)
    state = jnp.where(species, jnp.maximum(state, 0.0), state)

    def tail(value, a, b, c):
        a = jnp.where(row == SPECIES, a, jnp.where(row == SPECIES + 1, b, c))
        return jnp.where(species, value, a)

    def advance(s, state):
        w = state[SPECIES : SPECIES + 1]
        safe = jnp.maximum(state, FLOOR)
        high, rest = two_parts(jnp.log2(safe))
        middle, low = two_parts(rest)
        heat = jnp.tanh(w)
        heat_0, rest = two_parts(heat)
        heat_1, heat_2 = two_parts(rest)
        stacked = jnp.concatenate(
            [
                tail(high, heat_0, heat_1, 1.0),
                tail(middle, heat_0, 1.0, 1.0),
                tail(low, heat_1, heat_2, heat_0),
            ],
            axis=0,
        ).astype(BF16)
        p = jnp.exp2(jnp.dot(gathers[...], stacked, preferred_element_type=F32))
        high, low = two_parts(p)
        both = jnp.concatenate([high, low], axis=0).astype(BF16)
        totals = jnp.dot(sums[...], both, preferred_element_type=F32)
        gained = totals[:ROWS] + totals[ROWS : 2 * ROWS]
        lost = totals[2 * ROWS : 3 * ROWS]
        updated = safe * (state + h * gained) / (safe + h * lost)
        warm = jnp.concatenate([warming[...]] * GROUP, axis=1)
        rise = jnp.where(species, warm * (updated - state), 0.0)
        warmer = w + jnp.sum(rise, axis=0, keepdims=True)
        after = jnp.where(species, updated, jnp.broadcast_to(warmer, (ROWS, CELLS)))
        return jnp.where(s < number, after, state)

    turns = counts[ids[-1]]
    state = lax.fori_loop(0, turns, advance, state)
    for i in range(GROUP):
        place = (ids[i] & 1) * CX + (ids[i] >> 1)
        at = pl.multiple_of(place * ROWS, 8)
        done[pl.ds(at, ROWS), :] = state[:, i * 128 : i * 128 + 128]


def step_kernel(
    counts,
    order,
    above,
    own,
    below,
    edges_above,
    edges,
    edges_below,
    diffusion,
    gathers,
    sums,
    warming,
    species_out,
    warmth_out,
    slab,
    speeds,
    one,
    two,
    tiles,
    done,
):
    lane = lax.broadcasted_iota(jnp.int32, (8, 128), 1)

    def gather_rows(start, source, sides):
        def at_row(x, _):
            packed = sides[x]
            for t in range(FT):
                after = pltpu.roll(packed, (128 - 9 * t) % 128, 1)
                before = pltpu.roll(packed, (119 - 63 - 9 * t) % 128, 1)
                tile = jnp.where(lane < HALO, after, jnp.where(lane >= 128 - HALO, before, 0.0))
                value = jnp.concatenate([source[x, 2 * t], source[x, 2 * t + 1], tile], axis=1)
                slab[start + x, t] = value
                if t == FT - 1:
                    speeds[0, start + x] = jnp.broadcast_to(DT * value[6:7], (8, WIDE))
                    speeds[1, start + x] = jnp.broadcast_to(DT * value[7:8], (8, WIDE))
            return 0

        lax.fori_loop(0, source.shape[0], at_row, 0)

    gather_rows(0, above, edges_above)
    gather_rows(HALO, own, edges)
    gather_rows(HALO + CX, below, edges_below)

    def to_one(x, t, value):
        one[x, t] = value

    def to_two(x, t, value):
        two[x, t] = value

    def to_tiles(x, t, value):
        tiles[2 * x, t] = value[:, :128]
        tiles[2 * x + 1, t] = value[:, 128:256]

    run_stage(slab, None, 0, diffusion, speeds, 0, 44, 4, (None, None), to_one)
    run_stage(one, slab, 6, diffusion, speeds, 3, 40, 4, (0.75, 0.25), to_two)
    run_stage(two, slab, 9, diffusion, speeds, 6, 32, 4, (1.0 / 3.0, 2.0 / 3.0), to_tiles)

    def at_group(g, _):
        react_group(g, counts, order, tiles, gathers, sums, warming, done)
        return 0

    lax.fori_loop(0, TILES // GROUP, at_group, 0)

    for b in range(CX // 8):
        at = slice(b * 8, b * 8 + 8)
        for half in range(2):
            lanes = slice(half * 128, half * 128 + 128)
            row = (half * CX + b * 8) * ROWS
            for s in range(SPECIES):
                species_out[s, at, lanes] = done[pl.ds(row + s, 8, stride=ROWS), :]
            warmth_out[at, lanes] = done[pl.ds(row + SPECIES, 8, stride=ROWS), :]


def parts(value, number):
    out = []
    for _ in range(number):
        out.append(lax.reduce_precision(value, 8, 7))
        value = value - out[-1]
    return out


def tables(pairs, exponents, energies, output, diffusion, warming):
    extra = RXN - pairs.shape[0]
    padded = jnp.pad(pairs, ((0, extra), (0, 0)), constant_values=-1)
    ids = jnp.arange(SPECIES, dtype=jnp.int32)
    taken = (padded[:, :1] == ids).astype(F32) + (padded[:, 1:] == ids).astype(F32)
    scale = 1.0 / math.log(2.0)
    a = parts(jnp.pad(scale * exponents, (0, extra)), 3)
    e = parts(jnp.pad(scale * energies, (0, extra)), 3)
    tails = [(e[0], e[0], a[0]), (e[1], a[1], a[2]), (e[1], e[0], e[2])]
    gathers = jnp.concatenate([v for tail in tails for v in (taken, jnp.stack(tail, 1))], 1)
    high, low = parts(jnp.pad(output, ((0, extra), (0, ROWS - SPECIES))).T, 2)
    lost = jnp.pad(taken, ((0, 0), (0, ROWS - SPECIES))).T
    sums = jnp.concatenate([high, low, lost, jnp.zeros((8, RXN), F32)], 0)
    sums = jnp.concatenate([sums, sums], 1)

    def column(values):
        values = jnp.pad(values, (0, ROWS - values.shape[0]))
        return jnp.broadcast_to(values[:, None], (ROWS, 128))

    return (column(diffusion).reshape(FT, 8, 128), gathers.astype(BF16), sums.astype(BF16), column(warming))


def ranked(counts):
    number = jnp.arange(TILES, dtype=jnp.int32)
    key = counts * TILES + number
    rank = jnp.sum((key[None, :] < key[:, None]).astype(jnp.int32), axis=1)
    return jnp.sum(jnp.where(rank[None, :] == number[:, None], number[None, :], 0), axis=1)


def neighbours(axis):
    n = lax.axis_size(axis)
    up = [(i, (i + 1) % n) for i in range(n)]
    return up, [(j, i) for i, j in up]


VMEM = pl.BlockSpec(memory_space=pltpu.VMEM)
SMEM = pl.BlockSpec(memory_space=pltpu.SMEM)


def body(density, thermal, lead, trail, diffusion, pairs, exponents, energies, output, warming, counts):
    own, first, last, edges = pl.pallas_call(
        pack_kernel,
        out_shape=(
            jax.ShapeDtypeStruct((CX * 112, 128), F32),
            jax.ShapeDtypeStruct((HALO * 112, 128), F32),
            jax.ShapeDtypeStruct((HALO * 112, 128), F32),
            jax.ShapeDtypeStruct((CX, 8, 128), F32),
        ),
        in_specs=[VMEM] * 4,
        out_specs=(VMEM,) * 4,
        compiler_params=pltpu.CompilerParams(vmem_limit_bytes=16 * 2**20),
        name="pack",
    )(density, thermal, lead, trail)
    up, down = neighbours("grp")
    before = lax.ppermute(edges, "grp", up)
    after = lax.ppermute(edges, "grp", down)
    up, down = neighbours("gx")
    above = lax.ppermute(last, "gx", up)
    below = lax.ppermute(first, "gx", down)
    lane = jnp.arange(128, dtype=jnp.int32)
    sides = jnp.where(lane < 63, after, before)
    sides_above = lax.ppermute(sides[CX - HALO :], "gx", up)
    sides_below = lax.ppermute(sides[:HALO], "gx", down)
    consts = tables(pairs, exponents, energies, output, diffusion, warming)
    return pl.pallas_call(
        step_kernel,
        out_shape=(
            jax.ShapeDtypeStruct((SPECIES, CX, CY), F32),
            jax.ShapeDtypeStruct((CX, CY), F32),
        ),
        in_specs=[SMEM] * 2 + [VMEM] * 10,
        out_specs=(VMEM, VMEM),
        scratch_shapes=[
            pltpu.VMEM((CX + 18, FT, 8, WIDE), F32),
            pltpu.VMEM((2, CX + 18, 8, WIDE), F32),
            pltpu.VMEM((46, FT, 8, WIDE), F32),
            pltpu.VMEM((40, FT, 8, WIDE), F32),
            pltpu.VMEM((TILES, FT, 8, 128), F32),
            pltpu.VMEM((TILES * ROWS, 128), F32),
        ],
        compiler_params=pltpu.CompilerParams(vmem_limit_bytes=50 * 2**20),
        name="transport_and_chemistry",
    )(
        counts,
        ranked(counts),
        above.reshape(HALO, 14, 8, 128),
        own.reshape(CX, 14, 8, 128),
        below.reshape(HALO, 14, 8, 128),
        sides_above,
        sides,
        sides_below,
        *consts,
    )


def solution(mesh):
    return jax.shard_map(
        body,
        mesh=mesh,
        in_specs=(
            P(None, "gx", "grp"),
            P("gx", "grp"),
            P("gx", "grp"),
            P("gx", "grp"),
            P(),
            P(),
            P(),
            P(),
            P(),
            P(),
            P(("grp", "gx")),
        ),
        out_specs=(P(None, "gx", "grp"), P("gx", "grp")),
        check_vma=False,
    )
```

time: 498 us -> 74.3 us (0.15)
  the two profiles are of different devices: /device:TPU:97 before, /device:TPU:64 now
where the time goes in v1:
time: 74.3 us; the launch traced here: 73.5 us
  Pallas kernels  51.1 us (69%)
  local copies, waits for them, and re-layouts  11.5 us (15%)
  starting transfers between devices  9.25 us (12%)
  between operations  0.94 us (1%)
    pallas_call x1, Pallas kernels, body(): pl.pallas_call(step_kernel, out_shape=(jax.ShapeDtypeStruct((SPECIES, CX,...  48.1 us
    concatenate x2, local copies, waits for them, and re-layouts, tables(): jnp.concatenate([v for tail in tails for v in (taken, jnp.stack(tail, 1))...  6.77 us
    ppermute x1, starting transfers between devices, body(): below = lax.ppermute(first, 'gx', down)  5.06 us
    unnamed x22, local copies, waits for them, and re-layouts  3.76 us
    pallas_call x1, Pallas kernels, body(): pl.pallas_call(pack_kernel, out_shape=(jax.ShapeDtypeStruct((CX * 112, 12...  3.07 us
    ppermute x1, starting transfers between devices, body(): sides_below = lax.ppermute(sides[:HALO], 'gx', down)  2.15 us
    ppermute x1, starting transfers between devices, body(): before = lax.ppermute(edges, 'grp', up)  1.62 us
  transfers between devices with their start and end apart: 6, of which 0 were waited for; matrix products, arithmetic and copies ran while one was open for 11% of the time, Pallas kernels for 0%

profile of v1, /device:TPU:64, one launch (start us, length us, event | category | flops | bytes accessed | tf_op | source)
XLA Modules:
  0.0 73.5 jit_solution(2326544570753780684)
XLA Ops:
  0.6 0.0 copy-start
  0.6 1.5 %copy-done = f32[53,32,256]{2,1,0:T(8,128)S(1)} copy-done((f32[53,32,256]{2,1,0:T(8,128)S(1)}, f32[53,32,256]{2,1,0:T(8,128)}, u32[]{:S(2)}) %copy-start) | copy-done | bytes 1736728
  2.1 0.0 copy-start.1
  2.1 0.8 %copy-done.1 = f32[32,256]{1,0:T(8,128)S(1)} copy-done((f32[32,256]{1,0:T(8,128)S(1)}, f32[32,256]{1,0:T(8,128)}, u32[]{:S(2)}) %copy-start.1) | copy-done | bytes 32792
  2.9 0.0 copy-start.2
  2.9 0.8 %copy-done.2 = f32[32,256]{1,0:T(8,128)S(1)} copy-done((f32[32,256]{1,0:T(8,128)S(1)}, f32[32,256]{1,0:T(8,128)}, u32[]{:S(2)}) %copy-start.2) | copy-done | bytes 32792
  3.6 0.0 copy-start.3
  3.6 0.8 %copy-done.3 = f32[32,256]{1,0:T(8,128)S(1)} copy-done((f32[32,256]{1,0:T(8,128)S(1)}, f32[32,256]{1,0:T(8,128)}, u32[]{:S(2)}) %copy-start.3) | copy-done | bytes 32792
  4.4 0.0 copy-start.6
  4.4 0.0 copy-start.4
  4.4 0.0 copy-start.7
  4.4 0.0 copy-start.8
  4.4 0.0 copy-start.5
  4.4 0.0 copy-start.9
  4.4 0.0 copy-start.10
  4.4 3.1 %pack.1 = (f32[3584,128]{1,0:T(8,128)S(1)}, f32[1008,128]{1,0:T(8,128)}, f32[1008,128]{1,0:T(8,128)}, f32[32,8,128]{2,1,0:T(8,128)S(1)}) custom-call(f32[53,32,256]{2,1,0:T(8,128)S(1)} %copy-done, f32[32,256]{1,0:T(8,128)S(1)} %copy-done.1, f32[32,256]{1,0:T(8,128)S(1)} %copy-done.2, f32[32,256]{1,0:T(8,128)S(1)} %copy-done.3), custom_call_target="tpu_custom_call" | custom-call | tf_op jit(solution)/shard_map/pack/pallas_call | solution.py:264
  7.5 1.6 %collective-permute-start.3 = (f32[32,8,128]{2,1,0:T(8,128)S(1)}, f32[32,8,128]{2,1,0:T(8,128)S(1)}, u32[]{:S(2)}, u32[]{:S(2)}) collective-permute-start(f32[32,8,128]{2,1,0:T(8,128)S(1)} %get-tuple-element.9), channel_id=1, source_target_pairs={{0,32},{32,64},{64,96},{96,0},{1,33},{33,65},{65,97},{97,1},{2,34}... | collective-permute-start | bytes 393224 | tf_op jit(solution)/shard_map/ppermute | solution.py:278
  9.1 0.4 collective-permute-start.2
  9.5 0.0 collective-permute-start
  9.5 5.1 %collective-permute-start.1 = (f32[1008,128]{1,0:T(8,128)}, f32[1008,128]{1,0:T(8,128)S(1)}, u32[]{:S(2)}, u32[]{:S(2)}) collective-permute-start(f32[1008,128]{1,0:T(8,128)} %get-tuple-element.8), channel_id=1, source_target_pairs={{1,0},{2,1},{3,2},{4,3},{5,4},{6,5},{7,6},{8,7},{9,8},{10,9},{11,1... | collective-permute-start | bytes 1548296 | tf_op jit(solution)/shard_map/ppermute | solution.py:282
  14.6 0.0 copy-done.6
  14.7 0.0 copy-done.4
  14.7 0.2 convert_reduce_fusion
  14.9 0.1 select_reduce_fusion.order
  15.0 0.0 copy-done.7
  15.0 0.0 copy-done.8
  15.1 0.0 copy-done.5
  15.1 0.1 pad.39.clone
  15.2 0.1 maximum_convert_fusion
  15.3 0.1 pad_maximum_fusion.sums
  15.4 0.0 collective-permute-done.3
  15.4 0.0 collective-permute-done.2
  15.5 0.6 fusion.8
  16.1 2.2 %collective-permute-start.5 = (f32[9,8,128]{2,1,0:T(8,128)}, f32[9,8,128]{2,1,0:T(8,128)S(1)}, u32[]{:S(2)}, u32[]{:S(2)}) collective-permute-start(f32[9,8,128]{2,1,0:T(8,128)} %get-tuple-element.12), channel_id=1, source_target_pairs={{1,0},{2,1},{3,2},{4,3},{5,4},{6,5},{7,6},{8,7},{9,8},{10,9},{11,1... | collective-permute-start | bytes 110600 | tf_op jit(solution)/shard_map/ppermute | solution.py:286
  18.2 0.0 collective-permute-start.4
  18.3 0.0 copy-done.9
  18.3 0.0 copy-done.10
  18.4 0.1 broadcast_in_dim.43
  18.5 5.7 %concatenate.11 = bf16[336,168]{0,1:T(8,128)(2,1)} concatenate(bf16[336,53]{0,1:T(8,128)(2,1)S(1)} %fusion.1, bf16[336,1]{0,1:T(2,128)(2,1)S(1)} %reshape.27, bf16[336,1]{0,1:T(2,128)(2,1)S(1)} %reshape.27, bf16[336,1]{0,1:T(2,128)(2,1)S(1)} %stack.26, bf16[336,53]{0,1:T(8,128)(2,1)S(1)} %fusion.1, bf16[336,1]{0,1:T(2,128)(2,1)S(1)} %reshape.28, bf16[336,1]{0,1:T(2,128)(2,1)S(1)} %stack.28, ...), dimensions={1} | concatenate | bytes 225792 | tf_op jit(solution)/shard_map/concatenate | solution.py:233
  24.2 1.0 %copy.14.gathers = bf16[336,168]{1,0:T(8,128)(2,1)S(1)} copy(bf16[336,168]{0,1:T(8,128)(2,1)} %concatenate.11) | data formatting | bytes 225792 | tf_op jit(solution)/shard_map/concatenate | solution.py:233
  25.2 0.0 collective-permute-done.5.edges_below
  25.2 0.0 collective-permute-done.4.edges_above
  25.2 0.0 collective-permute-done
  25.3 0.0 collective-permute-done.1
  25.3 0.1 broadcast_in_dim.44.diffusion
  25.3 0.1 broadcast_in_dim.46.warming
  25.4 48.1 %transport_and_chemistry.1 = (f32[53,32,256]{2,1,0:T(8,128)}, f32[32,256]{1,0:T(8,128)}) custom-call(s32[64]{0:T(128)S(1)} %copy-done.4, s32[64]{0:T(128)S(1)} %select_reduce_fusion.order, f32[9,14,8,128]{3,2,1,0:T(8,128)S(1)} %bitcast.13, f32[32,14,8,128]{3,2,1,0:T(8,128)S(1)} %bitcast.12, f32[9,14,8,128]{3,2,1,0:T(8,128)S(1)} %bitcast.14, ...), custom_call_target="tpu_custom_call" | custom-call | tf_op jit(solution)/shard_map/transport_and_chemistry/pallas_call | solution.py:288
  (21 shorter events, 0.2 us)
Async XLA Ops:
  0.6 1.5 %copy-start = (f32[53,32,256]{2,1,0:T(8,128)S(1)}, f32[53,32,256]{2,1,0:T(8,128)}, u32[]{:S(2)}) copy-start(f32[53,32,256]{2,1,0:T(8,128)} %density.1) | copy-start | bytes 5210116
  2.1 0.8 %copy-start.1 = (f32[32,256]{1,0:T(8,128)S(1)}, f32[32,256]{1,0:T(8,128)}, u32[]{:S(2)}) copy-start(f32[32,256]{1,0:T(8,128)} %thermal.1) | copy-start | bytes 98308
  2.9 0.8 %copy-start.2 = (f32[32,256]{1,0:T(8,128)S(1)}, f32[32,256]{1,0:T(8,128)}, u32[]{:S(2)}) copy-start(f32[32,256]{1,0:T(8,128)} %lead.1) | copy-start | bytes 98308
  3.6 0.8 %copy-start.3 = (f32[32,256]{1,0:T(8,128)S(1)}, f32[32,256]{1,0:T(8,128)}, u32[]{:S(2)}) copy-start(f32[32,256]{1,0:T(8,128)} %trail.1) | copy-start | bytes 98308
  4.4 10.2 %copy-start.6 = (s32[325,2]{0,1:T(2,128)S(1)}, s32[325,2]{0,1:T(2,128)}, u32[]{:S(2)}) copy-start(s32[325,2]{0,1:T(2,128)} %param.16) | copy-start | bytes 7804
  4.4 10.3 %copy-start.4 = (s32[64]{0:T(128)S(1)}, s32[64]{0:T(128)}, u32[]{:S(2)}) copy-start(s32[64]{0:T(128)} %counts.1) | copy-start | bytes 772
  4.4 10.6 %copy-start.7 = (f32[325]{0:T(512)S(1)}, f32[325]{0:T(512)}, u32[]{:S(2)}) copy-start(f32[325]{0:T(512)} %param.17) | copy-start | bytes 3904
  4.4 10.6 %copy-start.8 = (f32[325]{0:T(512)S(1)}, f32[325]{0:T(512)}, u32[]{:S(2)}) copy-start(f32[325]{0:T(512)} %param.18) | copy-start | bytes 3904
  4.4 10.7 %copy-start.5 = (f32[325,53]{0,1:T(8,128)S(1)}, f32[325,53]{0,1:T(8,128)}, u32[]{:S(2)}) copy-start(f32[325,53]{0,1:T(8,128)} %param.19) | copy-start | bytes 206704
  4.4 13.9 %copy-start.9 = (f32[54]{0:T(128)S(1)}, f32[54]{0:T(128)}, u32[]{:S(2)}) copy-start(f32[54]{0:T(128)} %param.15) | copy-start | bytes 652
  4.4 13.9 %copy-start.10 = (f32[53]{0:T(128)S(1)}, f32[53]{0:T(128)}, u32[]{:S(2)}) copy-start(f32[53]{0:T(128)} %param.20) | copy-start | bytes 640
  7.5 7.9 %collective-permute-start.3 = (f32[32,8,128]{2,1,0:T(8,128)S(1)}, f32[32,8,128]{2,1,0:T(8,128)S(1)}, u32[]{:S(2)}, u32[]{:S(2)}) collective-permute-start(f32[32,8,128]{2,1,0:T(8,128)S(1)} %get-tuple-element.9), channel_id=1, source_target_pairs={{0,32},{32,64},{64,96},{96,0},{1,33},{33,65},{65,97},{97,1},{2,34}... | collective-permute-start | bytes 393224 | tf_op jit(solution)/shard_map/ppermute | solution.py:278
  9.1 6.3 %collective-permute-start.2 = (f32[32,8,128]{2,1,0:T(8,128)S(1)}, f32[32,8,128]{2,1,0:T(8,128)S(1)}, u32[]{:S(2)}, u32[]{:S(2)}) collective-permute-start(f32[32,8,128]{2,1,0:T(8,128)S(1)} %get-tuple-element.9), channel_id=1, source_target_pairs={{32,0},{64,32},{96,64},{0,96},{33,1},{65,33},{97,65},{1,97},{34,2}... | collective-permute-start | bytes 393224 | tf_op jit(solution)/shard_map/ppermute | solution.py:279
  9.5 15.7 %collective-permute-start = (f32[1008,128]{1,0:T(8,128)}, f32[1008,128]{1,0:T(8,128)S(1)}, u32[]{:S(2)}, u32[]{:S(2)}) collective-permute-start(f32[1008,128]{1,0:T(8,128)} %get-tuple-element.6), channel_id=1, source_target_pairs={{0,1},{1,2},{2,3},{3,4},{4,5},{5,6},{6,7},{7,8},{8,9},{9,10},{10,1... | collective-permute-start | bytes 1548296 | tf_op jit(solution)/shard_map/ppermute | solution.py:281
  9.5 15.7 %collective-permute-start.1 = (f32[1008,128]{1,0:T(8,128)}, f32[1008,128]{1,0:T(8,128)S(1)}, u32[]{:S(2)}, u32[]{:S(2)}) collective-permute-start(f32[1008,128]{1,0:T(8,128)} %get-tuple-element.8), channel_id=1, source_target_pairs={{1,0},{2,1},{3,2},{4,3},{5,4},{6,5},{7,6},{8,7},{9,8},{10,9},{11,1... | collective-permute-start | bytes 1548296 | tf_op jit(solution)/shard_map/ppermute | solution.py:282
  16.1 9.1 %collective-permute-start.5 = (f32[9,8,128]{2,1,0:T(8,128)}, f32[9,8,128]{2,1,0:T(8,128)S(1)}, u32[]{:S(2)}, u32[]{:S(2)}) collective-permute-start(f32[9,8,128]{2,1,0:T(8,128)} %get-tuple-element.12), channel_id=1, source_target_pairs={{1,0},{2,1},{3,2},{4,3},{5,4},{6,5},{7,6},{8,7},{9,8},{10,9},{11,1... | collective-permute-start | bytes 110600 | tf_op jit(solution)/shard_map/ppermute | solution.py:286
  18.2 7.0 %collective-permute-start.4 = (f32[9,8,128]{2,1,0:T(8,128)}, f32[9,8,128]{2,1,0:T(8,128)S(1)}, u32[]{:S(2)}, u32[]{:S(2)}) collective-permute-start(f32[9,8,128]{2,1,0:T(8,128)} %get-tuple-element.13), channel_id=1, source_target_pairs={{0,1},{1,2},{2,3},{3,4},{4,5},{5,6},{6,7},{7,8},{8,9},{9,10},{10,1... | collective-permute-start | bytes 110600 | tf_op jit(solution)/shard_map/ppermute | solution.py:285
